TPU v7x, 32 devices: a whole 2x2x4 slice. The times are simulated.
32 devices in a mesh: groups: 2 (over y), expert: 8 (over z, core), tensor: 1, side: 2 (over x).
Axes of the slice: x: 2, y: 2, z: 4, core: 2. Of those that a mesh axis runs over, the one named last changes fastest.
Arguments:
- queries: bfloat16 [128, 64, 576], P(('groups', 'expert')), parts along dimension 0, may hold values from -30 to 30
- latent_cache: bfloat16 [128, 1024, 576], P(('groups', 'expert'), ('tensor', 'side')), parts along dimension 0, may hold values from -5 to 5
- lengths: int32 [128], P(('groups', 'expert')), parts along dimension 0, may hold values from 2 to 1024, as said below
- assignment: int32 [128], P('groups'), parts along dimension 0, may hold values from 0 to 63, each once
- w_uv: bfloat16 [64, 512, 128], P(('tensor', 'side')), may hold values from -0.25 to 0.25
- w_o: bfloat16 [8192, 3584], P(('tensor', 'side'), 'expert'), may hold values from -0.26367188 to 0.26367188
- residual: bfloat16 [128, 3584], P('groups', 'expert'), parts along dimension 0, may hold values from -3 to 3
- gain: bfloat16 [3584], P('expert'), may hold values from 0.099609375 to 1.8984375
- expert_ids: int32 [128, 8], P('groups'), parts along dimension 0, may hold values from 0 to 15, all different within a row; in each aligned block of 64 rows (0 to 63, 64 to 127, ...) at most 64 rows name the same one
- expert_weights: float32 [128, 8], P('groups'), parts along dimension 0, may hold values from 0.1 to 1
- w_gate: bfloat16 [16, 3584, 1024], P(('expert', 'side'), None, 'tensor'), may hold values from -0.09375 to 0.09375
- w_up: bfloat16 [16, 3584, 1024], P(('expert', 'side'), None, 'tensor'), may hold values from -0.09375 to 0.09375
- w_down: bfloat16 [16, 1024, 3584], P(('expert', 'side'), 'tensor'), may hold values from -0.1875 to 0.1875
Outputs:
- layer_out: float32 [128, 3584], P('groups', 'expert'), parts along dimension 0
There are 2 independent parts, one for each index of `groups`. A program takes and returns all parts, laid end to end along the dimension named above; an argument that names none is the same for every part. Nothing has to cross between parts.
Inputs may be any that keep to these rules, and one draw needn't show every extreme that they name: `lengths`: each request's cache is filled at positions below its length; some request has exactly 1024. `expert_ids`: no expert is chosen by more than 64 tokens, and some expert is chosen by exactly 64.
All inputs are finite; a program needn't handle non-finite values.
Results may differ from a plain program's by a relative error of at most 0.0037.
The roundings to bfloat16 on the way count: a program that leaves them out, or rounds other values in their place, can miss the bound.
Values may be sent and summed in bfloat16 or wider, within the bound.
A program may use at most 128 MiB of HBM per device.

v0:
```python
import jax
import jax.numpy as jnp
from jax import lax
from jax.sharding import PartitionSpec as P

score_scale = 0.07216878364870323
neg_large = -1e30


def joined_2(part, axis, combine):
    gathered = jax.tree.map(lambda a: lax.all_gather(a, axis), part)

    def take(source):
        return jax.tree.map(lambda a: lax.dynamic_index_in_dim(a, source, 0, False), gathered)

    return lax.fori_loop(
        1, lax.axis_size(axis), lambda source, state: combine(state, take(source)), take(0)
    )


def softmax_join(first_part, second_part):
    first_max, first_sum, first_acc = first_part
    second_max, second_sum, second_acc = second_part
    joint_max = jnp.maximum(first_max, second_max)
    first_factor = jnp.exp(first_max - joint_max)
    second_factor = jnp.exp(second_max - joint_max)
    joint_sum = first_sum * first_factor + second_sum * second_factor
    joint_acc = first_acc * first_factor[..., None] + second_acc * second_factor[..., None]
    return (joint_max, joint_sum, joint_acc)


def shards(
    queries,
    latent_cache,
    lengths,
    assignment,
    w_uv,
    w_o,
    residual,
    gain,
    expert_ids,
    expert_weights,
    w_gate,
    w_up,
    w_down,
):
    highest = lax.Precision.HIGHEST
    req_rows = queries.shape[0]
    span_len = latent_cache.shape[1]
    lat_width = w_uv.shape[1]
    own_heads = w_uv.shape[0]
    head_group = lax.axis_index(("tensor", "side"))
    position_start = head_group * span_len
    scores = (
        jnp.einsum("rhc,rpc->rhp", queries, latent_cache, preferred_element_type=jnp.float32)
        * score_scale
    )
    places = position_start + lax.broadcasted_iota(jnp.int32, (req_rows, 1, span_len), 2)
    in_range = places < lengths[:, None, None]
    scores = jnp.where(in_range, scores, neg_large)
    top_score = jnp.max(scores, axis=2)
    weight_rows = jnp.where(in_range, jnp.exp(scores - top_score[..., None]), 0.0)
    weight_sum = jnp.sum(weight_rows, axis=2)
    cache_values = latent_cache[:, :, :lat_width].astype(jnp.float32)
    weighted = jnp.einsum("rhp,rpc->rhc", weight_rows, cache_values, precision=highest)
    joined = joined_2((top_score, weight_sum, weighted), ("tensor", "side"), softmax_join)
    head_start = head_group * own_heads
    weight_sum = lax.dynamic_slice_in_dim(joined[1], head_start, own_heads, 1)
    weighted = lax.dynamic_slice_in_dim(joined[2], head_start, own_heads, 1)
    latent_out = (weighted / weight_sum[..., None]).astype(jnp.bfloat16)
    head_values = jnp.einsum(
        "rhc,hcv->rhv", latent_out, w_uv, preferred_element_type=jnp.float32
    ).astype(jnp.bfloat16)
    head_values = head_values.reshape(req_rows, own_heads * w_uv.shape[2])
    slot_terms = jnp.dot(
        lax.all_gather(head_values, "expert", axis=0, tiled=True),
        w_o,
        preferred_element_type=jnp.float32,
    )
    token_count = slot_terms.shape[0]
    request_slot = (
        jnp.zeros((token_count,), jnp.int32)
        .at[assignment]
        .set(jnp.arange(token_count, dtype=jnp.int32))
    )
    attention = lax.psum(slot_terms[request_slot], ("tensor", "side"))
    hidden_state = residual.astype(jnp.float32) + attention
    squares = lax.psum(jnp.sum(hidden_state * hidden_state, axis=1), "expert")
    model_width = w_gate.shape[1]
    normed = (
        hidden_state * lax.rsqrt(squares / model_width + 1e-06)[:, None] * gain.astype(jnp.float32)
    ).astype(jnp.bfloat16)
    top_count = expert_ids.shape[1]
    expert_tally = lax.axis_size("expert")
    side_count = lax.axis_size("side")
    side_index = lax.axis_index("side")
    all_experts = expert_tally * side_count
    capacity = min(token_count, 2 * token_count * top_count // all_experts)
    flat_ids = expert_ids.reshape(-1)
    hits = (flat_ids[:, None] == jnp.arange(all_experts, dtype=jnp.int32)[None, :]).astype(
        jnp.int32
    )
    earlier = jnp.cumsum(hits, axis=0) - hits
    slot_index = jnp.sum(earlier * hits, axis=1)
    own_side = flat_ids % side_count == side_index
    rows_at = jnp.where(
        own_side, flat_ids // side_count * capacity + slot_index, expert_tally * capacity
    )
    owners = jnp.repeat(jnp.arange(token_count, dtype=jnp.int32), top_count)
    slot_owner = (
        jnp.full((expert_tally * capacity,), -1, jnp.int32).at[rows_at].set(owners, mode="drop")
    )
    filled = slot_owner >= 0
    outgoing = jnp.where(
        filled[:, None], normed[jnp.maximum(slot_owner, 0)], jnp.zeros((), jnp.bfloat16)
    )
    outgoing = outgoing.reshape(expert_tally, capacity, normed.shape[1])
    arrived_rows = lax.all_to_all(outgoing, "expert", split_axis=0, concat_axis=2, tiled=True)[0]
    gate_output = jnp.dot(arrived_rows, w_gate[0], preferred_element_type=jnp.float32)
    up_out = jnp.dot(arrived_rows, w_up[0], preferred_element_type=jnp.float32)
    hidden_units = (jax.nn.silu(gate_output) * up_out).astype(jnp.bfloat16)
    partial_rows = jnp.dot(hidden_units, w_down[0], preferred_element_type=jnp.float32)
    summed = lax.psum(partial_rows.astype(jnp.bfloat16), "tensor").astype(jnp.float32)
    sent_back = lax.all_to_all(
        summed[None].astype(jnp.bfloat16), "expert", split_axis=2, concat_axis=0, tiled=True
    ).astype(jnp.float32)
    flat_returned = sent_back.reshape(expert_tally * capacity, sent_back.shape[2])
    picked = flat_returned[jnp.minimum(rows_at, expert_tally * capacity - 1)]
    picked = picked.reshape(token_count, top_count, sent_back.shape[2])
    route_scale = jnp.where(own_side, expert_weights.reshape(-1), 0.0).reshape(
        token_count, top_count
    )
    expert_mix = jnp.einsum("tk,tkd->td", route_scale, picked, precision=highest)
    expert_mix = lax.psum(expert_mix.astype(jnp.bfloat16), "side").astype(jnp.float32)
    return hidden_state + expert_mix


def solution(mesh):
    in_specs = (
        P(("groups", "expert"), None, None),
        P(("groups", "expert"), ("tensor", "side"), None),
        P(("groups", "expert")),
        P("groups"),
        P(("tensor", "side"), None, None),
        P(("tensor", "side"), "expert"),
        P("groups", "expert"),
        P("expert"),
        P("groups", None),
        P("groups", None),
        P(("expert", "side"), None, "tensor"),
        P(("expert", "side"), None, "tensor"),
        P(("expert", "side"), "tensor", None),
    )
    out_specs = P("groups", "expert")
    return jax.shard_map(shards, mesh=mesh, in_specs=in_specs, out_specs=out_specs, check_vma=False)
```

profile of v0, /device:TPU:0, one launch (start us, length us, event | category | flops | bytes accessed | tf_op | source)
XLA Modules:
  0.0 209.6 jit_solution(4113221504775275167)
XLA Ops:
  6.5 0.9 broadcast_compare_fusion
  7.6 3.9 %fusion.58 = (f32[8,64]{1,0:T(8,128)S(1)}, f32[8,64,512]{2,1,0:T(8,128)S(1)}) fusion(bf16[8,64,576]{2,1,0:T(8,128)(2,1)S(1)} %copy-done, bf16[8,512,576]{1,2,0:T(8,128)(2,1)} %param.14, pred[8,512]{1,0:T(8,128)(4,1)S(1)} %broadcast_compare_fusion), kind=kOutput, calls=%fused_computation.96 | convolution fusion | flops 302775808 | bytes 6363136 | tf_op jit(solution)/shard_map/rhc,rpc->rhp/dot_general | solution.py:55
  11.5 4.9 %fusion.12 = f32[8,64,512]{2,1,0:T(8,128)} fusion(bf16[8,512,576]{1,2,0:T(8,128)(2,1)S(1)} %copy-done.1, f32[8,64,512]{2,1,0:T(8,128)S(1)} %get-tuple-element.37, f32[8,64]{1,0:T(8,128)S(1)} %get-tuple-element.36, pred[8,512]{1,0:T(8,128)(4,1)S(1)} %broadcast_compare_fusion), kind=kOutput, calls=%fused_computation.13 | convolution fusion | flops 1611137024 | bytes 6299648 | tf_op jit(solution)/shard_map/rhp,rpc->rhc/dot_general | solution.py:65
  16.9 1.2 reduce-window.6
  18.4 0.8 scatter_custom_fusion
  19.4 2.4 %scatter_custom_fusion.1 = s32[512]{0:T(512)S(1)} fusion(s32[512]{0:T(512)S(1)} %bitcast.82, s32[512]{0:T(512)S(1)} %reshape.292, s32[]{:T(128)} %constant.92.clone.1), kind=kCustom, calls=%fused_computation.88 | custom fusion | bytes 2052 | tf_op jit(solution)/shard_map/scatter | solution.py:111
  21.8 5.2 %all-gather.1 = f32[16,64]{1,0:T(8,128)S(1)} all-gather(f32[8,64]{1,0:T(8,128)S(1)} %get-tuple-element.36), channel_id=3, replica_groups=mesh['groups'=2,'expert'=8,'tensor'=1,'side'=2] {'tensor','side'}, dimensions={0}, use_global_device_ids=true | all-gather | bytes 6144 | tf_op jit(solution)/shard_map/all_gather | solution.py:11
  27.4 4.4 %all-gather.2 = f32[16,64]{1,0:T(8,128)S(1)} all-gather(f32[8,64]{1,0:T(8,128)S(1)} %fusion.22), channel_id=4, replica_groups=mesh['groups'=2,'expert'=8,'tensor'=1,'side'=2] {'tensor','side'}, dimensions={0}, use_global_device_ids=true | all-gather | bytes 6144 | tf_op jit(solution)/shard_map/all_gather | solution.py:11
  31.9 20.5 %all-gather.5.cloned.1.call-done = f32[16,64,512]{2,1,0:T(8,128)} async-done(((f32[8,64,512]{2,1,0:T(8,128)}), f32[16,64,512]{2,1,0:T(8,128)}) %all-gather.5.cloned.1.call-update) | async-done | bytes 2097168 | tf_op jit(solution)/shard_map/all_gather | solution.py:11
  52.5 1.9 fusion.57
  54.6 0.7 copy-done.2
  55.3 0.7 fusion.21
  56.0 14.8 %all_gather.27 = bf16[64,4096]{1,0:T(8,128)(2,1)S(1)} all-gather(bf16[8,4096]{1,0:T(8,128)(2,1)S(1)} %fusion.21), channel_id=1, replica_groups=mesh['groups'=2,'expert'=8,'tensor'=1,'side'=2] {'expert'}, dimensions={0}, use_global_device_ids=true | all-gather | bytes 589824 | tf_op jit(solution)/shard_map/all_gather | solution.py:76
  70.8 1.2 fusion.59
  72.0 1.3 gather_fusion
  73.4 21.6 %all-reduce.2.cloned.1.call-done = f32[64,448]{1,0:T(8,128)} async-done(((f32[64,448]{1,0:T(8,128)}), f32[64,448]{1,0:T(8,128)}) %all-reduce.2.cloned.1.call-update) | async-done | bytes 114704 | tf_op jit(solution)/shard_map/psum | solution.py:86
  95.1 1.0 multiply_reduce_fusion
  96.1 15.9 %psum.25 = f32[64]{0:T(128)S(1)} all-reduce(f32[64]{0:T(128)S(1)} %multiply_reduce_fusion), channel_id=1, replica_groups=mesh['groups'=2,'expert'=8,'tensor'=1,'side'=2] {'expert'}, use_global_device_ids=true, to_apply=%region_9.10 | all-reduce | flops 64 | bytes 512 | tf_op jit(solution)/shard_map/psum | solution.py:88
  112.0 1.0 multiply_convert_fusion
  113.0 2.0 gather_fusion.1
  115.1 17.8 %all_to_all.30 = bf16[8,64,448]{2,1,0:T(8,128)(2,1)S(1)} all-to-all(bf16[8,64,448]{2,1,0:T(8,128)(2,1)S(1)} %broadcast_select_fusion), channel_id=1, replica_groups=mesh['groups'=2,'expert'=8,'tensor'=1,'side'=2] {'expert'}, dimensions={0} | all-to-all | bytes 917504 | tf_op jit(solution)/shard_map/all_to_all | solution.py:118
  133.8 4.5 %fusion.4 = f32[64,1024]{1,0:T(8,128)S(1)} fusion(bf16[64,3584]{1,0:T(8,128)(2,1)S(1)} %squeeze.41, bf16[1,3584,1024]{2,1,0:T(8,128)(2,1)} %param.23), kind=kOutput, calls=%fused_computation.9 | convolution fusion | flops 469762048 | bytes 8060928 | tf_op jit(solution)/shard_map/dot_general | solution.py:119
  138.2 7.9 %fusion.9 = bf16[1,64,3584]{2,1,0:T(8,128)(2,1)S(1)} fusion(bf16[1,1024,3584]{2,1,0:T(8,128)(2,1)} %param.25, bf16[64,3584]{1,0:T(8,128)(2,1)S(1)} %squeeze.41, bf16[1,3584,1024]{2,1,0:T(8,128)(2,1)} %param.24, f32[64,1024]{1,0:T(8,128)S(1)} %fusion.4), kind=kOutput, calls=%fused_computation.12 | convolution fusion | flops 940146688 | bytes 15859712 | tf_op jit(solution)/shard_map/dot_general | solution.py:122
  146.1 2.5 %copy.50 = bf16[1,64,3584]{1,0,2:T(2,128)(2,1)S(1)} copy(bf16[1,64,3584]{2,1,0:T(8,128)(2,1)S(1)} %fusion.9) | data formatting | bytes 917504 | tf_op jit(solution)/shard_map/convert_element_type | solution.py:125
  149.1 19.7 %reduce.2 = bf16[3584,64]{1,0:T(8,128)(2,1)S(1)} reduce(bf16[3584,1,64]{2,1,0:T(2,128)(2,1)S(1)} %bitcast.74, bf16[]{:T(256)} %broadcast.283), dimensions={1}, to_apply=%bitcast.61.reduce_sub_computation | reduce | bytes 917506
  168.8 1.4 reshape.321
  170.2 3.5 %all-to-all-start.1 = ((bf16[8,2,14336]{2,1,0:T(2,128)(2,1)}), bf16[8,2,14336]{2,1,0:T(2,128)(2,1)S(1)}, u32[]{:S(2)}, u32[]{:S(2)}) async-start(bf16[8,2,14336]{2,1,0:T(2,128)(2,1)} %reshape.321), calls=%async_computation.1 | async-start | bytes 917504 | tf_op jit(solution)/shard_map/all_to_all | solution.py:124
  173.8 13.8 %all-to-all-done.1 = bf16[8,2,14336]{2,1,0:T(2,128)(2,1)S(1)} async-done(((bf16[8,2,14336]{2,1,0:T(2,128)(2,1)}), bf16[8,2,14336]{2,1,0:T(2,128)(2,1)S(1)}, u32[]{:S(2)}, u32[]{:S(2)}) %all-to-all-start.1) | async-done | bytes 458784 | tf_op jit(solution)/shard_map/all_to_all | solution.py:124
  187.6 1.2 reshape.322
  188.7 2.1 copy.51
  191.6 2.0 gather_fusion.2
  194.2 7.9 %psum.26 = bf16[64,448]{1,0:T(8,128)(2,1)S(1)} all-reduce(bf16[64,448]{1,0:T(8,128)(2,1)S(1)} %bitcast.79), channel_id=1, replica_groups=mesh['groups'=2,'expert'=8,'tensor'=1,'side'=2] {'side'}, use_global_device_ids=true, to_apply=%region_10.11 | all-reduce | flops 28672 | bytes 114688 | tf_op jit(solution)/shard_map/psum | solution.py:134
  (64 shorter events, 5.6 us)
Async XLA Ops:
  6.5 1.1 copy-start
  6.5 45.9 %all-gather.5.cloned.1.call-start = ((), (), s32[]{:S(2)}) async-start(), calls=%async_computation.3 | async-start | bytes 3145728 | tf_op jit(solution)/shard_map/all_gather | solution.py:11
  6.5 5.0 %copy-start.1 = (bf16[8,512,576]{1,2,0:T(8,128)(2,1)S(1)}, bf16[8,512,576]{1,2,0:T(8,128)(2,1)}, u32[]{:S(2)}) copy-start(bf16[8,512,576]{1,2,0:T(8,128)(2,1)} %param.14) | copy-start | bytes 14155780
  11.5 5.0 %copy-start.6 = (s32[64,8]{0,1:T(8,128)S(1)}, s32[64,8]{0,1:T(8,128)}, u32[]{:S(2)}) copy-start(s32[64,8]{0,1:T(8,128)} %param.21) | copy-start | bytes 6148
  11.5 6.9 %copy-start.9 = (s32[64]{0:T(128)S(1)}, s32[64]{0:T(128)}, u32[]{:S(2)}) copy-start(s32[64]{0:T(128)} %param.16) | copy-start | bytes 772
  16.5 78.6 %all-reduce.2.cloned.1.call-start = ((), (), s32[]{:S(2)}) async-start(), calls=%async_computation.2 | async-start | bytes 262144 | tf_op jit(solution)/shard_map/psum | solution.py:86
  52.5 2.8 %copy-start.2 = (bf16[32,512,128]{2,1,0:T(8,128)(2,1)S(1)}, bf16[32,512,128]{2,1,0:T(8,128)(2,1)}, u32[]{:S(2)}) copy-start(bf16[32,512,128]{2,1,0:T(8,128)(2,1)} %param.17) | copy-start | bytes 12582916
  52.5 18.3 %copy-start.3 = (bf16[4096,448]{0,1:T(8,128)(2,1)S(1)}, bf16[4096,448]{0,1:T(8,128)(2,1)}, u32[]{:S(2)}) copy-start(bf16[4096,448]{0,1:T(8,128)(2,1)} %param.18) | copy-start | bytes 11010052
  55.3 18.0 %copy-start.8 = (bf16[448]{0:T(512)(128)(2,1)S(1)}, bf16[448]{0:T(512)(128)(2,1)}, u32[]{:S(2)}) copy-start(bf16[448]{0:T(512)(128)(2,1)} %param.20) | copy-start | bytes 2692
  55.3 39.8 %copy-start.5 = (bf16[64,448]{1,0:T(8,128)(2,1)S(1)}, bf16[64,448]{1,0:T(8,128)(2,1)}, u32[]{:S(2)}) copy-start(bf16[64,448]{1,0:T(8,128)(2,1)} %param.19) | copy-start | bytes 172036
  146.1 27.6 %copy-start.7 = (f32[64,8]{0,1:T(8,128)S(1)}, f32[64,8]{0,1:T(8,128)}, u32[]{:S(2)}) copy-start(f32[64,8]{0,1:T(8,128)} %param.22) | copy-start | bytes 6148
  170.2 17.4 %all-to-all-start.1 = ((bf16[8,2,14336]{2,1,0:T(2,128)(2,1)}), bf16[8,2,14336]{2,1,0:T(2,128)(2,1)S(1)}, u32[]{:S(2)}, u32[]{:S(2)}) async-start(bf16[8,2,14336]{2,1,0:T(2,128)(2,1)} %reshape.321), calls=%async_computation.1 | async-start | bytes 917504 | tf_op jit(solution)/shard_map/all_to_all | solution.py:124
  188.7 13.3 %copy-start.4 = (f32[64,448]{1,0:T(8,128)S(1)}, f32[64,448]{1,0:T(8,128)}, u32[]{:S(2)}) copy-start(f32[64,448]{1,0:T(8,128)} %all-reduce.2.cloned.1.call-done) | copy-start | bytes 344068
Sparse Core Ops, SparseCore 0:
  16.6 35.8 all-gather.4
  73.4 21.5 all-reduce.1
where the time goes:
time: 210 us
  blocking collectives  66 us (31%)
  waiting for transfers between devices  55.9 us (27%)
  other arithmetic  25.3 us (12%)
  matrix products  23.5 us (11%)
  local copies, waits for them, and re-layouts  21.6 us (10%)
  between operations  13.7 us (7%)
  starting transfers between devices  3.52 us (2%)
    psum x1, waiting for transfers between devices, shards(): attention = lax.psum(slot_terms[request_slot], ('tensor', 'side'))  21.6 us
    all_gather x1, waiting for transfers between devices, joined_2(): gathered = jax.tree.map(lambda a: lax.all_gather(a, axis), part)  20.5 us
    unnamed x1, other arithmetic  19.7 us
    all_to_all x1, blocking collectives, shards(): lax.all_to_all(outgoing, 'expert', split_axis=0, concat_axis=2, tiled=True)  17.8 us
    psum x1, blocking collectives, shards(): squares = lax.psum(jnp.sum(hidden_state * hidden_state, axis=1), 'expert')  15.9 us
    all_gather x1, blocking collectives, shards(): lax.all_gather(head_values, 'expert', axis=0, tiled=True)  14.8 us
    all_to_all x1, waiting for transfers between devices, shards(): lax.all_to_all(summed[None].astype(jnp.bfloat16), 'expert', split_axis=2,...  13.8 us
    all_gather x2, blocking collectives, joined_2(): gathered = jax.tree.map(lambda a: lax.all_gather(a, axis), part)  9.59 us
  transfers between devices with their start and end apart: 3, of which 3 were waited for; matrix products, arithmetic and copies ran while one was open for 3% of the time, Pallas kernels for 0%

commit v1 on v0

--- a/solution.py
+++ b/solution.py
@@ -1,10 +1,13 @@
 import jax
 import jax.numpy as jnp
 from jax import lax
+from jax.experimental import pallas as pl
+from jax.experimental.pallas import tpu as pltpu
 from jax.sharding import PartitionSpec as P
 
 score_scale = 0.07216878364870323
 neg_large = -1e30
+MESH = pl.DeviceIdType.MESH
 
 
 def joined_2(part, axis, combine):
@@ -135,6 +138,420 @@
     return hidden_state + expert_mix
 
 
+def layer_kernel(
+    lengths,
+    assignment,
+    residual,
+    gain,
+    expert_ids,
+    expert_weights,
+    queries_hbm,
+    cache_hbm,
+    w_uv_hbm,
+    w_o_hbm,
+    w_gate_hbm,
+    w_up_hbm,
+    w_down_hbm,
+    out,
+    queries,
+    cache,
+    w_uv,
+    w_o,
+    w_gate,
+    w_up,
+    w_down,
+    own_acc,
+    stats_own,
+    stats_send,
+    stats_recv,
+    lat_send,
+    lat_recv,
+    latent,
+    head_wide,
+    head_all,
+    part_send,
+    part_recv,
+    hidden,
+    scaled_all,
+    gate_acc,
+    up_acc,
+    kept,
+    give,
+    got,
+    mix_send,
+    mix_recv,
+    last_send,
+    last_recv,
+    load_sem,
+    lat_sems,
+    stat_sems,
+    head_sems,
+    part_sems,
+    row_sems,
+    got_sems,
+    mix_sems,
+    last_sems,
+):
+    f32, bf16 = jnp.float32, jnp.bfloat16
+    requests, all_heads, _ = queries.shape
+    span = cache.shape[1]
+    own_heads, lat_width, v_width = w_uv.shape
+    half = own_heads // 2
+    tokens, block = residual.shape
+    model_width = w_gate.shape[0]
+    devices = model_width // block
+    chips = devices // 2
+    me = lax.axis_index("expert")
+    side = lax.axis_index("side")
+    core = lax.rem(me, 2)
+    chip = lax.div(me, 2)
+    sibling = {"expert": chip * 2 + 1 - core}
+    across = {"side": 1 - side}
+
+    def chip_at(step):
+        return lax.rem(chip + step, chips)
+
+    def on_chip(step):
+        return {"expert": chip_at(step) * 2 + core}
+
+    loads = [
+        pltpu.make_async_copy(source, target, load_sem.at[i])
+        for i, (source, target) in enumerate(
+            [
+                (queries_hbm, queries),
+                (w_uv_hbm, w_uv),
+                (w_o_hbm, w_o),
+                (w_gate_hbm, w_gate),
+                (w_up_hbm, w_up),
+                (w_down_hbm, w_down),
+            ]
+        )
+    ]
+    cache_loads = [
+        pltpu.make_async_copy(cache_hbm.at[r], cache.at[r], load_sem.at[len(loads) + r])
+        for r in range(requests)
+    ]
+    loads[0].start()
+    for r in range(requests):
+        cache_loads[r].start()
+    for load in loads[1:]:
+        load.start()
+
+    barrier = pltpu.get_barrier_semaphore()
+    partners = [sibling, across] + [on_chip(step) for step in range(1, chips)]
+    for partner in partners:
+        pl.semaphore_signal(barrier, inc=1, device_id=partner, device_id_type=MESH)
+    pl.semaphore_wait(barrier, len(partners))
+
+    def send(source, target, sems, index, where):
+        return pltpu.make_async_remote_copy(
+            src_ref=source,
+            dst_ref=target,
+            send_sem=sems.at[0, index],
+            recv_sem=sems.at[1, index],
+            device_id=where,
+            device_id_type=MESH,
+        )
+
+    places = side * span + lax.broadcasted_iota(jnp.int32, (all_heads, span), 1)
+    lanes = lax.broadcasted_iota(jnp.int32, (all_heads, 128), 1)
+    stats = jnp.zeros((all_heads, 128), f32)
+    own_rows = pl.ds(pl.multiple_of(side * own_heads, own_heads), own_heads)
+    other_rows = pl.ds(pl.multiple_of((1 - side) * own_heads, own_heads), own_heads)
+    loads[0].wait()
+    lat_copies = []
+    for r in range(requests):
+        cache_loads[r].wait()
+        q = jnp.concatenate([queries[r, own_rows, :], queries[r, other_rows, :]], axis=0)
+        scores = lax.dot_general(
+            q, cache[r], (((1,), (1,)), ((), ())), preferred_element_type=f32
+        )
+        in_range = places < lengths[r]
+        scores = jnp.where(in_range, scores * score_scale, neg_large)
+        top = jnp.max(scores, axis=1, keepdims=True)
+        weights = jnp.where(in_range, jnp.exp(scores - top), 0.0)
+        total = jnp.sum(weights, axis=1, keepdims=True)
+        high = weights.astype(bf16)
+        low = (weights - high.astype(f32)).astype(bf16)
+        acc = jnp.dot(
+            jnp.concatenate([high, low], axis=0),
+            cache[r, :, :lat_width],
+            preferred_element_type=f32,
+        )
+        acc = acc[:all_heads] + acc[all_heads:]
+        stats = jnp.where(lanes == 2 * r, top, jnp.where(lanes == 2 * r + 1, total, stats))
+        own_acc[r] = acc[:own_heads]
+        other_total = total[own_heads:]
+        lat_send[r] = jnp.where(
+            other_total > 0.0, acc[own_heads:] / jnp.maximum(other_total, 1e-30), 0.0
+        ).astype(bf16)
+        copy = send(lat_send.at[r], lat_recv.at[r], lat_sems, r, across)
+        copy.start()
+        lat_copies.append(copy)
+    stats_own[...] = stats[:own_heads]
+    stats_send[...] = stats[own_heads:]
+    stat_copy = send(stats_send, stats_recv, stat_sems, 0, across)
+    stat_copy.start()
+
+    stat_copy.wait_recv()
+    first = stats_own[...]
+    second = stats_recv[...]
+    for r in range(requests):
+        first_top, first_sum = first[:, 2 * r : 2 * r + 1], first[:, 2 * r + 1 : 2 * r + 2]
+        second_top, second_sum = second[:, 2 * r : 2 * r + 1], second[:, 2 * r + 1 : 2 * r + 2]
+        joint = jnp.maximum(first_top, second_top)
+        first_factor = jnp.exp(first_top - joint)
+        second_factor = jnp.exp(second_top - joint) * second_sum
+        inverse = 1.0 / (first_sum * first_factor + second_factor)
+        lat_copies[r].wait_recv()
+        latent[r] = own_acc[r] * (first_factor * inverse) + lat_recv[r].astype(f32) * (
+            second_factor * inverse
+        )
+
+    loads[1].wait()
+    for h in range(own_heads):
+        rows = latent[:, h, :].astype(bf16)
+        head_wide[
+            (h // half) * requests : (h // half + 1) * requests,
+            (h % half) * v_width : (h % half + 1) * v_width,
+        ] = jnp.dot(rows, w_uv[h], preferred_element_type=f32)
+    pair_rows = 2 * requests
+
+    def head_slot(device):
+        return head_all.at[pl.ds(pl.multiple_of(device * pair_rows, pair_rows), pair_rows), :]
+
+    def row_slot(device):
+        return scaled_all.at[pl.ds(pl.multiple_of(device * tokens, tokens), tokens), :]
+
+    def gather(slot, sems):
+        far = [
+            send(slot(me), slot(me), sems, step - 1, on_chip(step)) for step in range(1, chips)
+        ]
+        near = [send(slot(me), slot(me), sems, chips - 1, sibling)]
+        for copy in far + near:
+            copy.start()
+        for step in range(1, chips):
+            near.append(
+                send(
+                    slot(chip_at(chips - step) * 2 + core),
+                    slot(chip_at(chips - step) * 2 + core),
+                    sems,
+                    chips - 1 + step,
+                    sibling,
+                )
+            )
+        return far, near
+
+    head_slot(me)[...] = head_wide[...].astype(bf16)
+    far, near = gather(head_slot, head_sems)
+    for step in range(1, chips):
+        far[step - 1].wait_recv()
+        near[step].start()
+    for step in range(chips):
+        near[step].wait_recv()
+    head_copies = far + near
+    loads[2].wait()
+    depth = half * v_width
+    first_term = jnp.dot(head_all[...], w_o[:depth, :], preferred_element_type=f32)
+    second_term = jnp.dot(head_all[...], w_o[depth:, :], preferred_element_type=f32)
+    slot_terms = (
+        first_term.reshape(devices, 2, requests, block)[:, 0]
+        + second_term.reshape(devices, 2, requests, block)[:, 1]
+    ).reshape(tokens, block)
+    order = (
+        lax.broadcasted_iota(jnp.int32, (tokens, tokens), 0) == assignment[...]
+    ).astype(f32).astype(bf16)
+    part_send[...] = jnp.dot(
+        order, slot_terms.astype(bf16), preferred_element_type=f32
+    ).astype(bf16)
+    part_copy = send(part_send, part_recv, part_sems, 0, across)
+    part_copy.start()
+    base = residual[...].astype(f32)
+    scale = gain[...].astype(f32)
+    part_copy.wait_recv()
+    state = base + (part_send[...].astype(f32) + part_recv[...].astype(f32))
+    hidden[...] = state
+    squares = jnp.sum(state * state, axis=1, keepdims=True)
+    sq_high = squares.astype(bf16).astype(f32)
+    sq_mid = (squares - sq_high).astype(bf16).astype(f32)
+    sq_low = squares - sq_high - sq_mid
+    extra = scaled_all.shape[1] - block
+    extra_lanes = lax.broadcasted_iota(jnp.int32, (tokens, extra), 1)
+    tail = jnp.where(
+        extra_lanes == 0,
+        sq_high,
+        jnp.where(extra_lanes == 1, sq_mid, jnp.where(extra_lanes == 2, sq_low, 0.0)),
+    )
+    row_slot(me)[...] = jnp.concatenate([state * scale, tail], axis=1).astype(bf16)
+    far, near = gather(row_slot, row_sems)
+    row_copies = far + near
+
+    loads[3].wait()
+    loads[4].wait()
+    square_sum = jnp.zeros((tokens, 1), f32)
+
+    def absorb(device, begin, square_sum):
+        rows = row_slot(device)[...]
+        part = rows[:, :block]
+        weight_rows = pl.ds(pl.multiple_of(device * block, 64), block)
+        gate_part = jnp.dot(part, w_gate[weight_rows, :], preferred_element_type=f32)
+        up_part = jnp.dot(part, w_up[weight_rows, :], preferred_element_type=f32)
+        if begin:
+            gate_acc[...] = gate_part
+            up_acc[...] = up_part
+        else:
+            gate_acc[...] += gate_part
+            up_acc[...] += up_part
+        return square_sum + jnp.sum(rows[:, block:].astype(f32), axis=1, keepdims=True)
+
+    square_sum = absorb(me, True, square_sum)
+    near[0].wait_recv()
+    square_sum = absorb(chip * 2 + 1 - core, False, square_sum)
+    for step in (1, 3, 2) if chips == 4 else range(1, chips):
+        far[step - 1].wait_recv()
+        near[step].start()
+        square_sum = absorb(chip_at(chips - step) * 2 + core, False, square_sum)
+        near[step].wait_recv()
+        square_sum = absorb(chip_at(chips - step) * 2 + 1 - core, False, square_sum)
+    norm = lax.rsqrt(square_sum / model_width + 1e-06)
+    gate_output = gate_acc[...] * norm
+    units = (gate_output * jax.nn.sigmoid(gate_output) * (up_acc[...] * norm)).astype(bf16)
+
+    expert = me * 2 + side
+    route = jnp.sum(
+        jnp.where(expert_ids[...] == expert, expert_weights[...], 0.0), axis=1, keepdims=True
+    )
+    loads[5].wait()
+    got_copies, mix_copies = [], []
+
+    def forward(step):
+        got_copies[step].wait_recv()
+        both = kept[step] + got[step].astype(f32)
+        if step == chips - 1:
+            return both
+        mix_send[step] = both.astype(bf16)
+        copy = send(mix_send.at[step], mix_recv.at[step], mix_sems, step, on_chip(step + 1))
+        copy.start()
+        mix_copies.append(copy)
+
+    for step in range(chips):
+        columns = pl.ds(pl.multiple_of(chip_at(step + 1) * (2 * block), 128), 2 * block)
+        result = jnp.dot(units, w_down[:, columns], preferred_element_type=f32) * route
+        left, right = result[:, :block], result[:, block:]
+        kept[step] = jnp.where(core == 0, left, right)
+        give[step] = jnp.where(core == 0, right, left).astype(bf16)
+        copy = send(give.at[step], got.at[step], got_sems, step, sibling)
+        copy.start()
+        got_copies.append(copy)
+        if step:
+            forward(step - 1)
+    mixed = forward(chips - 1)
+    for step in range(chips - 1):
+        mix_copies[step].wait_recv()
+        mixed = mixed + mix_recv[step].astype(f32)
+    last_send[...] = mixed.astype(bf16)
+    last_copy = send(last_send, last_recv, last_sems, 0, across)
+    last_copy.start()
+    last_copy.wait_recv()
+    out[...] = hidden[...] + (last_send[...].astype(f32) + last_recv[...].astype(f32))
+    for copy in (
+        lat_copies + [stat_copy] + head_copies + [part_copy] + row_copies + got_copies
+        + mix_copies + [last_copy]
+    ):
+        copy.wait_send()
+
+
+def fused(
+    queries,
+    latent_cache,
+    lengths,
+    assignment,
+    w_uv,
+    w_o,
+    residual,
+    gain,
+    expert_ids,
+    expert_weights,
+    w_gate,
+    w_up,
+    w_down,
+):
+    f32, bf16 = jnp.float32, jnp.bfloat16
+    requests = queries.shape[0]
+    own_heads, lat_width, v_width = w_uv.shape
+    tokens, block = residual.shape
+    model_width, units = w_gate.shape[1:]
+    chips = model_width // block // 2
+    wide = -(-(block + 3) // 128) * 128
+    vmem = pl.BlockSpec(memory_space=pltpu.VMEM)
+    hbm = pl.BlockSpec(memory_space=pl.ANY)
+    buffer = pltpu.VMEM
+    pairs = pltpu.SemaphoreType.DMA
+    return pl.pallas_call(
+        layer_kernel,
+        out_shape=jax.ShapeDtypeStruct((tokens, block), f32),
+        in_specs=[pl.BlockSpec(memory_space=pltpu.SMEM)] + [vmem] * 5 + [hbm] * 7,
+        out_specs=vmem,
+        scratch_shapes=[
+            buffer(queries.shape, bf16),
+            buffer(latent_cache.shape, bf16),
+            buffer(w_uv.shape, bf16),
+            buffer(w_o.shape, bf16),
+            buffer((model_width, units), bf16),
+            buffer((model_width, units), bf16),
+            buffer((units, model_width), bf16),
+            buffer((requests, own_heads, lat_width), f32),
+            buffer((own_heads, 128), f32),
+            buffer((own_heads, 128), f32),
+            buffer((own_heads, 128), f32),
+            buffer((requests, own_heads, lat_width), bf16),
+            buffer((requests, own_heads, lat_width), bf16),
+            buffer((requests, own_heads, lat_width), f32),
+            buffer((2 * requests, own_heads * v_width // 2), f32),
+            buffer((2 * tokens, own_heads * v_width // 2), bf16),
+            buffer((tokens, block), bf16),
+            buffer((tokens, block), bf16),
+            buffer((tokens, block), f32),
+            buffer((2 * chips * tokens, wide), bf16),
+            buffer((tokens, units), f32),
+            buffer((tokens, units), f32),
+            buffer((chips, tokens, block), f32),
+            buffer((chips, tokens, block), bf16),
+            buffer((chips, tokens, block), bf16),
+            buffer((chips - 1, tokens, block), bf16),
+            buffer((chips - 1, tokens, block), bf16),
+            buffer((tokens, block), bf16),
+            buffer((tokens, block), bf16),
+            pairs((6 + requests,)),
+            pairs((2, requests)),
+            pairs((2, 1)),
+            pairs((2, 2 * chips - 1)),
+            pairs((2, 1)),
+            pairs((2, 2 * chips - 1)),
+            pairs((2, chips)),
+            pairs((2, chips - 1)),
+            pairs((2, 1)),
+        ],
+        compiler_params=pltpu.CompilerParams(
+            collective_id=0, has_side_effects=True, vmem_limit_bytes=58 * 1024 * 1024
+        ),
+    )(
+        lengths,
+        assignment[None, :],
+        residual,
+        gain[None, :],
+        expert_ids,
+        expert_weights,
+        queries,
+        latent_cache,
+        w_uv,
+        w_o,
+        w_gate[0],
+        w_up[0],
+        w_down[0],
+    )
+
+
 def solution(mesh):
     in_specs = (
         P(("groups", "expert"), None, None),
@@ -152,4 +569,7 @@
         P(("expert", "side"), "tensor", None),
     )
     out_specs = P("groups", "expert")
-    return jax.shard_map(shards, mesh=mesh, in_specs=in_specs, out_specs=out_specs, check_vma=False)
+    sizes = mesh.shape
+    one_kernel = sizes["tensor"] == 1 and sizes["side"] == 2 and sizes["expert"] == 8
+    body = fused if one_kernel else shards
+    return jax.shard_map(body, mesh=mesh, in_specs=in_specs, out_specs=out_specs, check_vma=False)

time: 210 us -> 71 us (0.34)
  blocking collectives: 66 us -> 0 us
  waiting for transfers between devices: 55.9 us -> 0 us
  Pallas kernels: 0 us -> 50.7 us
  other arithmetic: 25.3 us -> 0 us
  matrix products: 23.5 us -> 0 us
  between operations: 13.7 us -> 0.01 us
  starting transfers between devices: 3.52 us -> 0 us
    pallas_call x0 -> x1, Pallas kernels: none -> 50.7 us  [fused(): pl.pallas_call(layer_kernel, out_shape=jax.ShapeDtypeStruct((tokens, bloc...]
    all_gather x3 -> x0, blocking collectives: 24.4 us -> none  [the longest x1 14.8 us: shards(): lax.all_gather(head_values, 'expert', axis=0, tiled=True)]
    psum x2 -> x0, blocking collectives: 23.8 us -> none  [the longest x1 15.9 us: shards(): squares = lax.psum(jnp.sum(hidden_state * hidden_state, axis=1), 'expert')]
    dot_general x7 -> x0, matrix products: 23.5 us -> none  [the longest x1 7.86 us: shards(): jnp.dot(hidden_units, w_down[0], preferred_element_type=jnp.float32)]
    psum x1 -> x0, waiting for transfers between devices: 21.6 us -> none  [shards(): attention = lax.psum(slot_terms[request_slot], ('tensor', 'side'))]
    all_gather x1 -> x0, waiting for transfers between devices: 20.5 us -> none  [joined_2(): gathered = jax.tree.map(lambda a: lax.all_gather(a, axis), part)]
    unnamed x1 -> x0, other arithmetic: 19.7 us -> none
    all_to_all x1 -> x0, blocking collectives: 17.8 us -> none  [shards(): lax.all_to_all(outgoing, 'expert', split_axis=0, concat_axis=2, tiled=True)]
  transfers between devices with their start and end apart: 3 -> 0, of which waited for: 3 -> 0; matrix products, arithmetic and copies ran while one was open for 3% -> 0% of each run, Pallas kernels for 0% -> 0%
where the time goes in v1:
time: 71 us; the launch traced here: 70.4 us
  Pallas kernels  50.7 us (71%)
  local copies, waits for them, and re-layouts  19.7 us (28%)
    pallas_call x1, Pallas kernels, fused(): pl.pallas_call(layer_kernel, out_shape=jax.ShapeDtypeStruct((tokens, bloc...  50.7 us
    unnamed x5, local copies, waits for them, and re-layouts  18.5 us

profile of v1, /device:TPU:0, one launch (start us, length us, event | category | flops | bytes accessed | tf_op | source)
XLA Modules:
  0.0 70.4 jit_solution(350568012274032364)
XLA Ops:
  0.0 1.3 %broadcast_in_dim.7.gain = bf16[1,448]{1,0:T(2,128)(2,1)} reshape(bf16[448]{0:T(512)(128)(2,1)} %param.20) | data formatting | bytes 1792 | tf_op jit(solution)/shard_map/broadcast_in_dim | solution.py:542
  1.3 1.4 %copy.14.expert_ids = s32[64,8]{1,0:T(8,128)} copy(s32[64,8]{0,1:T(8,128)} %param.21) | data formatting | bytes 4096 | tf_op args[8]
  2.7 1.4 %copy.15.expert_weights = f32[64,8]{1,0:T(8,128)} copy(f32[64,8]{0,1:T(8,128)} %param.22) | data formatting | bytes 4096 | tf_op args[9]
  4.0 6.5 %copy.17.w_o_hbm = bf16[4096,448]{1,0:T(8,128)(2,1)} copy(bf16[4096,448]{0,1:T(8,128)(2,1)} %param.18) | data formatting | bytes 7340032 | tf_op args[5]
  10.5 7.7 %copy.16.cache_hbm = bf16[8,512,576]{2,1,0:T(8,128)(2,1)} copy(bf16[8,512,576]{1,2,0:T(8,128)(2,1)} %param.14) | data formatting | bytes 9437184 | tf_op args[1]
  18.2 50.7 %shard_map.127 = f32[64,448]{1,0:T(8,128)} custom-call(s32[8]{0:T(128)} %lengths.1, s32[1,64]{1,0:T(1,128)} %bitcast.7, bf16[64,448]{1,0:T(8,128)(2,1)} %residual.1, bf16[1,448]{1,0:T(2,128)(2,1)} %broadcast_in_dim.7.gain, s32[64,8]{1,0:T(8,128)} %copy.14.expert_ids, f32[64,8]{1,0:T(8,128)} %copy.15.expert_weights, bf16[8,64,576]{2,1,0:T(8,128)(2,1)} %queries_hbm.1, ...), custom_call_target="tpu_custom_call" | custom-call | tf_op jit(solution)/shard_map/pallas_call | solution.py:490
  68.9 1.6 %copy.19 = f32[64,448]{1,0:T(8,128)} copy(f32[64,448]{1,0:T(8,128)} %shard_map.127) | data formatting | bytes 229376

commit v2 on v1

--- a/solution.py
+++ b/solution.py
@@ -194,7 +194,7 @@
 ):
     f32, bf16 = jnp.float32, jnp.bfloat16
     requests, all_heads, _ = queries.shape
-    span = cache.shape[1]
+    span = cache.shape[2]
     own_heads, lat_width, v_width = w_uv.shape
     half = own_heads // 2
     tokens, block = residual.shape
@@ -207,6 +207,11 @@
     chip = lax.div(me, 2)
     sibling = {"expert": chip * 2 + 1 - core}
     across = {"side": 1 - side}
+
+    def dot_turned(left, right):
+        return lax.dot_general(
+            left, right, (((1,), (1,)), ((), ())), preferred_element_type=f32
+        )
 
     def chip_at(step):
         return lax.rem(chip + step, chips)
@@ -263,9 +268,7 @@
     for r in range(requests):
         cache_loads[r].wait()
         q = jnp.concatenate([queries[r, own_rows, :], queries[r, other_rows, :]], axis=0)
-        scores = lax.dot_general(
-            q, cache[r], (((1,), (1,)), ((), ())), preferred_element_type=f32
-        )
+        scores = jnp.dot(q, cache[r], preferred_element_type=f32)
         in_range = places < lengths[r]
         scores = jnp.where(in_range, scores * score_scale, neg_large)
         top = jnp.max(scores, axis=1, keepdims=True)
@@ -273,11 +276,7 @@
         total = jnp.sum(weights, axis=1, keepdims=True)
         high = weights.astype(bf16)
         low = (weights - high.astype(f32)).astype(bf16)
-        acc = jnp.dot(
-            jnp.concatenate([high, low], axis=0),
-            cache[r, :, :lat_width],
-            preferred_element_type=f32,
-        )
+        acc = dot_turned(jnp.concatenate([high, low], axis=0), cache[r, :lat_width, :])
         acc = acc[:all_heads] + acc[all_heads:]
         stats = jnp.where(lanes == 2 * r, top, jnp.where(lanes == 2 * r + 1, total, stats))
         own_acc[r] = acc[:own_heads]
@@ -352,8 +351,8 @@
     head_copies = far + near
     loads[2].wait()
     depth = half * v_width
-    first_term = jnp.dot(head_all[...], w_o[:depth, :], preferred_element_type=f32)
-    second_term = jnp.dot(head_all[...], w_o[depth:, :], preferred_element_type=f32)
+    first_term = dot_turned(head_all[...], w_o[:, :depth])
+    second_term = dot_turned(head_all[...], w_o[:, depth:])
     slot_terms = (
         first_term.reshape(devices, 2, requests, block)[:, 0]
         + second_term.reshape(devices, 2, requests, block)[:, 1]
@@ -367,7 +366,7 @@
     part_copy = send(part_send, part_recv, part_sems, 0, across)
     part_copy.start()
     base = residual[...].astype(f32)
-    scale = gain[...].astype(f32)
+    scale = gain[...].astype(f32)[None, :]
     part_copy.wait_recv()
     state = base + (part_send[...].astype(f32) + part_recv[...].astype(f32))
     hidden[...] = state
@@ -418,9 +417,13 @@
     units = (gate_output * jax.nn.sigmoid(gate_output) * (up_acc[...] * norm)).astype(bf16)
 
     expert = me * 2 + side
-    route = jnp.sum(
-        jnp.where(expert_ids[...] == expert, expert_weights[...], 0.0), axis=1, keepdims=True
-    )
+    route_row = jnp.sum(
+        jnp.where(expert_ids[...] == expert, expert_weights[...], 0.0), axis=0, keepdims=True
+    )
+    diagonal = lax.broadcasted_iota(jnp.int32, (tokens, tokens), 0) == lax.broadcasted_iota(
+        jnp.int32, (tokens, tokens), 1
+    )
+    route = jnp.sum(jnp.where(diagonal, route_row, 0.0), axis=1, keepdims=True)
     loads[5].wait()
     got_copies, mix_copies = [], []
 
@@ -494,9 +497,9 @@
         out_specs=vmem,
         scratch_shapes=[
             buffer(queries.shape, bf16),
-            buffer(latent_cache.shape, bf16),
+            buffer((requests, latent_cache.shape[2], latent_cache.shape[1]), bf16),
             buffer(w_uv.shape, bf16),
-            buffer(w_o.shape, bf16),
+            buffer(w_o.shape[::-1], bf16),
             buffer((model_width, units), bf16),
             buffer((model_width, units), bf16),
             buffer((units, model_width), bf16),
@@ -539,13 +542,13 @@
         lengths,
         assignment[None, :],
         residual,
-        gain[None, :],
-        expert_ids,
-        expert_weights,
+        gain,
+        expert_ids.T,
+        expert_weights.T,
         queries,
-        latent_cache,
+        latent_cache.transpose(0, 2, 1),
         w_uv,
-        w_o,
+        w_o.T,
         w_gate[0],
         w_up[0],
         w_down[0],

time: 71 us -> 52.7 us (0.74)
  local copies, waits for them, and re-layouts: 19.7 us -> 1.57 us
    unnamed x5 -> x1, local copies, waits for them, and re-layouts: 18.5 us -> 1.57 us
    broadcast_in_dim x1 -> x0, local copies, waits for them, and re-layouts: 1.27 us -> none  [fused(): gain[None, :]]
where the time goes in v2:
time: 52.7 us; the launch traced here: 52.6 us
  Pallas kernels  51 us (97%)
  local copies, waits for them, and re-layouts  1.57 us (3%)
    pallas_call x1, Pallas kernels, fused(): pl.pallas_call(layer_kernel, out_shape=jax.ShapeDtypeStruct((tokens, bloc...  51 us
    unnamed x1, local copies, waits for them, and re-layouts  1.57 us

profile of v2, /device:TPU:0, one launch (start us, length us, event | category | flops | bytes accessed | tf_op | source)
XLA Modules:
  0.0 52.6 jit_solution(15081234931338018638)
XLA Ops:
  0.0 51.0 %shard_map.127 = f32[64,448]{1,0:T(8,128)} custom-call(s32[8]{0:T(128)} %lengths.1, s32[1,64]{1,0:T(1,128)} %bitcast.15, bf16[64,448]{1,0:T(8,128)(2,1)} %residual.1, bf16[448]{0:T(512)(128)(2,1)} %gain.1, s32[8,64]{1,0:T(8,128)} %bitcast.13, f32[8,64]{1,0:T(8,128)} %bitcast.14, bf16[8,64,576]{2,1,0:T(8,128)(2,1)} %queries_hbm.1, ...), custom_call_target="tpu_custom_call" | custom-call | tf_op jit(solution)/shard_map/pallas_call | solution.py:493
  51.0 1.6 %copy.15 = f32[64,448]{1,0:T(8,128)} copy(f32[64,448]{1,0:T(8,128)} %shard_map.127) | data formatting | bytes 229376
